TPU v7x, 128 devices: a whole 4x4x4 slice. The times are simulated.
128 devices in a mesh: gx: 16 (over x_hi, y, core), gy: 8 (over z, x_lo).
Axes of the slice: x: 4 (x_hi: 2, x_lo: 2; x = x_hi * 2 + x_lo), y: 4, z: 4, core: 2. Of those that a mesh axis runs over, the one named last changes fastest.
Arguments:
- incident: bfloat16 [6, 256, 128, 192], P(None, 'gx', 'gy'), may hold values from -6 to 6
- adjoint_source: bfloat16 [6, 256, 128, 192], P(None, 'gx', 'gy'), may hold values from -6 to 6
- cell_class: int32 [256, 128], P('gx', 'gy'), may hold values from 0 to 7
- slot_table: int32 [8, 8], replicated, may hold values from 0 to 7, each once within a row
- gain_table: float32 [8, 8, 192], replicated, may hold values from 0.3 to 1.5
- admittance: float32 [8, 192], replicated, may hold values from 0.5 to 1.5
- coupling: bfloat16 [8, 192, 192], replicated, may hold values from -0.109375 to 0.109375
- self_inverse: bfloat16 [192, 192], replicated, may hold values from -0.15 to 1.21
Outputs:
- current: bfloat16 [6, 256, 128, 192], P(None, 'gx', 'gy')
- adjoint_state: bfloat16 [6, 256, 128, 192], P(None, 'gx', 'gy')
All inputs are finite; a program needn't handle non-finite values.
Results may differ from a plain program's by a relative error of at most 0.02.
Values may be sent and summed in bfloat16 or wider, within the bound.
A program may use at most 128 MiB of HBM per device.

v0:
```python
import functools

import jax
import jax.numpy as jnp
from jax import lax
from jax.experimental import pallas as pl
from jax.experimental.pallas import tpu as pltpu
from jax.sharding import PartitionSpec as P

MESH = pl.DeviceIdType.MESH
F32 = jnp.float32
BF16 = jnp.bfloat16
SWEEPS = 3
R = 6
N = 16
ROWS = N * N
EDGE = R * N
U = 192
T = 128
HALF = 64
STEPS = ((-1, -1), (-1, 0), (-1, 1), (0, -1), (0, 1), (1, -1), (1, 0), (1, 1))
PAIRS = ((0, 5), (1, 6), (2, 7), (3, 4))
TILES = 12
Y_DIRS = ((0, 3, 5), (2, 4, 7))
X_DIRS = ((0, 1, 2), (5, 6, 7))
Y_TILES = ((0, 3, 5, 8, 11), (2, 4, 7, 10, 11))
X_TILES = ((0, 1, 2, 8, 9, 10), (5, 6, 7, 8, 9, 10))


def dot(a, b):
    return jnp.dot(a, b, preferred_element_type=F32)


def dot_nt(a, b):
    return lax.dot_general(a, b, (((1,), (1,)), ((), ())), preferred_element_type=F32)


def iota(shape, dim):
    return lax.broadcasted_iota(jnp.int32, shape, dim)


def low(rows):
    return iota((rows, T), 1) < HALF


def turn(x, shift, axis=0):
    size = x.shape[axis]
    return x if shift % size == 0 else pltpu.roll(x, shift % size, axis)


def spread(tile, corner=None):
    return jnp.concatenate([tile] * R + ([] if corner is None else [corner]), axis=0)


def fold(tile):
    return tile + turn(tile, HALF, 1)


def kernel(
    nx, ny,
    inc, src, cls, slot, gain, adm, coup, sinv,
    cur_out, adj_out,
    v0, vm, vp, adj, near_a, near_h, far_a, far_h, gains, lhs, weights, weights_t, partial,
    admit, admit_e, inc_e, src_e, gains_y, gains_x, solve, solve_t, solve_tn, corner_s,
    send_y, send_x, send_c, recv_y, recv_x, recv_c,
    send_sem, recv_sem,
):
    gx, gy = lax.axis_index("gx"), lax.axis_index("gy")
    left, right = lax.rem(gx + nx - 1, nx), lax.rem(gx + 1, nx)
    down, up = lax.rem(gy + ny - 1, ny), lax.rem(gy + 1, ny)
    y_to = ((gx, down), (gx, up))
    x_to = ((left, gy), (right, gy))
    c_to = ((left, down), (right, down), (left, up), (right, up))

    barrier = pltpu.get_barrier_semaphore()
    for where in y_to + x_to + c_to:
        pl.semaphore_signal(barrier, inc=1, device_id=where, device_id_type=MESH)

    one = jnp.float32(1.0)
    has_left, has_right = jnp.where(gx > 0, 1.0, 0.0) * one, jnp.where(gx < nx - 1, 1.0, 0.0) * one
    has_down, has_up = jnp.where(gy > 0, 1.0, 0.0) * one, jnp.where(gy < ny - 1, 1.0, 0.0) * one

    def chooser(rows, columns, wanted):
        return jnp.where(iota((rows, columns), 0) == wanted, 1.0, 0.0).astype(BF16)

    lane = iota((U, 2 * T), 1)
    dup = chooser(U, 2 * T, jnp.where(lane < U, lane, lane - HALF))
    dup_back = chooser(U, 2 * T, jnp.where(lane < HALF, lane + T, jnp.where(lane < T, lane + HALF, lane - T)))
    eye = chooser(U, U, iota((U, U), 1))
    solve[...] = dot(sinv[...], dup).astype(BF16)
    solve_n = dot_nt(eye, sinv[...]).astype(BF16)
    solve_tn[...] = solve_n
    solve_t[...] = dot(solve_n, dup_back).astype(BF16)

    weights[...] = jnp.zeros_like(weights)
    for d in range(8):
        weights[d * T:(d + 1) * T, 0:U] = coup[d, 0:T, :]
    for p, (d0, d1) in enumerate(PAIRS):
        base = (8 + p) * T
        weights[base:base + HALF, 0:U] = coup[d0, T:U, :]
        weights[base + HALF:base + T, 0:U] = coup[d1, T:U, :]
    row = iota((2 * T, U), 0)
    place = jnp.where(row < HALF, -1, jnp.where(row < T, row + HALF, row - T))
    order = jnp.where(iota((2 * T, U), 1) == place, 1.0, 0.0).astype(BF16)
    for t in range(TILES):
        weights_t[:, t * T:(t + 1) * T] = dot_nt(order, weights[t * T:(t + 1) * T, 0:U]).astype(BF16)

    pick = [
        jnp.where(iota((8, 64), 1) == iota((8, 64), 0) * 8 + slot[:, d:d + 1], 1.0, 0.0)
        for d in range(8)
    ]
    pick = jnp.concatenate(pick, axis=0).astype(BF16)
    gain_dup = dot(gain[...].astype(BF16), dup).astype(BF16)
    table64 = dot(pick, gain_dup)
    pieces = [table64[d * 8:(d + 1) * 8, 0:T] for d in range(8)]
    for d0, d1 in PAIRS:
        pieces.append(jnp.where(low(8), table64[d0 * 8:(d0 + 1) * 8, T:], table64[d1 * 8:(d1 + 1) * 8, T:]))
    table = jnp.concatenate(pieces, axis=1)
    table = jnp.concatenate([table, jnp.zeros_like(table)], axis=0).astype(BF16)
    adm_high = adm[...].astype(BF16).astype(F32)
    adm_both = jnp.concatenate([adm_high, adm[...] - adm_high], axis=0).astype(BF16)
    adm_table = dot(adm_both, dup).astype(BF16)

    diag = iota((N, N), 0) == iota((N, N), 1)
    spots = [jnp.where(diag, cls[x:x + 1, :].astype(F32), 0.0) for x in range(N)]
    kind = dot(jnp.concatenate(spots, axis=0).astype(BF16), jnp.ones((N, N), BF16))

    def onehot(kinds):
        which = lax.rem(iota((kinds.shape[0], N), 1), 8)
        return jnp.where(which.astype(F32) == kinds, 1.0, 0.0).astype(BF16)

    kind_e = jnp.concatenate(
        [
            jnp.broadcast_to(cls[:, 0:1].astype(F32), (N, N)),
            jnp.broadcast_to(cls[:, N - 1:N].astype(F32), (N, N)),
            kind[0:N],
            kind[ROWS - N:ROWS],
        ],
        axis=0,
    )
    hot, hot_e = onehot(kind), onehot(kind_e)
    admit[...] = dot(hot, adm_table)
    admit_e[...] = dot(hot_e, adm_table)

    def inside(rows, sx, sy):
        r = iota((rows, T), 0)
        x, y = r // N + sx, lax.rem(r, N) + sy
        return (x >= 0) & (x < N) & (y >= 0) & (y < N)

    for t in range(TILES):
        value = dot(hot, table[:, t * T:(t + 1) * T])
        if t < 8:
            keep = jnp.where(inside(ROWS, *STEPS[t]), 1.0, 0.0)
        else:
            d0, d1 = PAIRS[t - 8]
            keep = jnp.where(
                low(ROWS), jnp.where(inside(ROWS, *STEPS[d0]), 1.0, 0.0), jnp.where(inside(ROWS, *STEPS[d1]), 1.0, 0.0)
            )
        gains[:, t * T:(t + 1) * T] = (value * keep).astype(BF16)

    edge_gain = dot(hot_e, table)
    spot = iota((N, T), 0)

    def along(j):
        return jnp.where((spot + j >= 0) & (spot + j < N), 1.0, 0.0)

    lows = jnp.where(low(N), 1.0, 0.0)
    for e, exists in enumerate((has_down, has_up)):
        raw = edge_gain[e * N:(e + 1) * N]
        first = jnp.where(spot < 8, 1.0, 0.0)
        side = first * has_left + (1.0 - first) * has_right
        for k, t in enumerate(Y_TILES[e]):
            tile = raw[:, t * T:(t + 1) * T]
            ends = jnp.where(spot < 8, jnp.broadcast_to(tile[0:1], (N, T)), jnp.broadcast_to(tile[N - 1:N], (N, T)))
            if k < 3:
                keep = along(k - 1)
                corner = (first, 0.0 * first, 1.0 - first)[k]
            elif k == 3:
                keep = lows * along(-1) + (1.0 - lows) * along(1)
                corner = lows * first + (1.0 - lows) * (1.0 - first)
            else:
                keep = lows if e == 0 else 1.0 - lows
                corner = 0.0 * first
            gains_y[e, 0:N, k * T:(k + 1) * T] = tile * keep * exists
            gains_y[e, N:2 * N, k * T:(k + 1) * T] = ends * corner * side * exists
    for e, exists in enumerate((has_left, has_right)):
        raw = edge_gain[(2 + e) * N:(3 + e) * N]
        for k, t in enumerate(X_TILES[e]):
            keep = along(k % 3 - 1)
            if k >= 3:
                keep = keep * (lows if e == 0 else 1.0 - lows)
            gains_x[e, :, k * T:(k + 1) * T] = raw[:, t * T:(t + 1) * T] * keep * exists

    for data, a_ref, h_ref, e_ref in ((inc, near_a, near_h, inc_e), (src, far_a, far_h, src_e)):
        h_ref[...] = jnp.zeros_like(h_ref)
        for r in range(R):
            a_ref[r * ROWS:(r + 1) * ROWS, :] = data[r, :, 0:T].astype(F32)
            h_ref[r * ROWS:(r + 1) * ROWS, 0:HALF] = data[r, :, T:U].astype(F32)
        for k, ref in enumerate((a_ref, h_ref)):
            columns = slice(k * T, (k + 1) * T)
            for e in range(2):
                e_ref[e * EDGE:(e + 1) * EDGE, columns] = ref[pl.ds(e * (N - 1), EDGE, stride=N), :]
                for r in range(R):
                    at = (2 + e) * EDGE + r * N
                    start = r * ROWS + e * (ROWS - N)
                    e_ref[at:at + N, columns] = ref[start:start + N, :]
            ref[...] = jnp.zeros_like(ref)
    for ref in (v0, vm, vp):
        for r in range(R):
            ref[r, 0:N, :] = jnp.zeros((N, 2 * T), BF16)
            ref[r, (N + 1) * N:(N + 2) * N, :] = jnp.zeros((N, 2 * T), BF16)
    partial[0:N, :] = jnp.zeros((N, TILES * T), BF16)
    partial[(N + 1) * N:(N + 2) * N, :] = jnp.zeros((N, TILES * T), BF16)
    corner_s[...] = jnp.zeros_like(corner_s)

    def take(ref):
        parts = [ref[pl.ds(e * (N - 1), EDGE, stride=N), :] for e in range(2)]
        for e in range(2):
            for r in range(R):
                start = r * ROWS + e * (ROWS - N)
                parts.append(ref[start:start + N, :])
        return jnp.concatenate(parts, axis=0)

    def solve_edges(v):
        scale = jnp.concatenate([spread(admit_e[e * N:(e + 1) * N, :]) for e in range(4)], axis=0)
        near_e = jnp.concatenate([take(near_a), take(near_h)], axis=1)
        rest = (inc_e[...] - near_e).astype(BF16)
        cur_e = dot(rest[:, 0:U], solve[...]) * scale
        far_e = jnp.concatenate([take(far_a), take(far_h)], axis=1)
        back = ((src_e[...] - far_e) * scale).astype(BF16)
        adj_e = dot(back[:, 0:U], solve_t[...])

        for e in range(2):
            rows = slice(e * EDGE, (e + 1) * EDGE)
            corner_s[0, 0:EDGE, :] = cur_e[rows, 0:T]
            corner_s[1, 0:EDGE, :] = cur_e[rows, T:]
            corner_s[2, 0:EDGE, :] = adj_e[rows, 0:T]
            corner_s[3, 0:EDGE, :] = adj_e[rows, T:]
            cut = [
                jnp.concatenate([corner_s[k, pl.ds(0, 8, stride=N), :], corner_s[k, pl.ds(N - 1, 8, stride=N), :]], axis=0)
                for k in range(4)
            ]
            state = jnp.concatenate([adj_e[rows], jnp.concatenate(cut[2:], axis=1)], axis=0).astype(BF16)
            out = []
            for k, t in enumerate(Y_TILES[e]):
                gain_k = gains_y[e, :, k * T:(k + 1) * T]
                out.append(dot(state, weights_t[:, t * T:(t + 1) * T]) * spread(gain_k[0:N], gain_k[N:]))
            part_a = turn(out[0][:EDGE], -1) + out[1][:EDGE] + turn(out[2][:EDGE], 1)
            part_h = fold(
                jnp.where(low(EDGE), turn(out[3][:EDGE], -1), turn(out[3][:EDGE], 1)) + out[4][:EDGE]
            )
            tail_a = out[0][EDGE:] + out[1][EDGE:] + out[2][EDGE:]
            tail_h = fold(out[3][EDGE:] + out[4][EDGE:])
            message = jnp.concatenate(
                [cur_e[rows, 0:T], jnp.where(low(EDGE), cur_e[rows, T:], part_h), part_a], axis=1
            ).astype(BF16)
            send_y[v, e] = message.reshape(R, N, 3 * T)
            tail = jnp.concatenate([cut[0], jnp.where(low(N), cut[1], tail_h), tail_a], axis=1)
            send_c[v, 2 * e] = tail[0:8]
            send_c[v, 2 * e + 1] = tail[8:16]
        for e in range(2):
            rows = slice((2 + e) * EDGE, (3 + e) * EDGE)
            state = adj_e[rows].astype(BF16)
            out = []
            for k, t in enumerate(X_TILES[e]):
                out.append(dot(state, weights_t[:, t * T:(t + 1) * T]) * spread(gains_x[e, :, k * T:(k + 1) * T]))
            part_a = turn(out[0], -1) + out[1] + turn(out[2], 1)
            part_h = fold(turn(out[3], -1) + out[4] + turn(out[5], 1))
            message = jnp.concatenate(
                [cur_e[rows, 0:T], jnp.where(low(EDGE), cur_e[rows, T:], part_h), part_a], axis=1
            ).astype(BF16)
            send_x[v, e] = message.reshape(R, N, 3 * T)

    def copies(v):
        made = []
        for e in range(2):
            made.append((send_y.at[v, e], recv_y.at[v, 1 - e], y_to[e], e, 1 - e))
        for e in range(2):
            made.append((send_x.at[v, e], recv_x.at[v, 1 - e], x_to[e], 2 + e, 3 - e))
        for q in range(4):
            made.append((send_c.at[v, q], recv_c.at[v, 3 - q], c_to[q], 4 + q, 7 - q))
        return [
            pltpu.make_async_remote_copy(
                src_ref=a, dst_ref=b, send_sem=send_sem.at[v, s], recv_sem=recv_sem.at[v, t],
                device_id=where, device_id_type=MESH,
            )
            for a, b, where, s, t in made
        ]

    def right_sides(r):
        at = pl.ds(pl.multiple_of(r * ROWS, ROWS), ROWS)
        near = jnp.concatenate([near_a[at, :], near_h[at, 0:HALF]], axis=1)
        far = jnp.concatenate([far_a[at, :], far_h[at, 0:HALF]], axis=1)
        rest = (inc[r].astype(F32) - near).astype(BF16)
        back = ((src[r].astype(F32) - far) * admit[:, 0:U]).astype(BF16)
        return rest, back

    def solve_block(r, carry):
        rest, back = right_sides(r)
        cur = dot(rest, solve[...]) * admit[...]
        v0[r, N:N + ROWS, :] = cur.astype(BF16)
        vm[r, N:N + ROWS, :] = turn(cur, 1).astype(BF16)
        vp[r, N:N + ROWS, :] = turn(cur, -1).astype(BF16)
        adj[r] = dot(back, solve_t[...]).astype(BF16)
        return carry

    shifted = {-1: vm, 0: v0, 1: vp}

    def near_block(r, carry):
        def nearby(d, columns):
            sx, sy = STEPS[d]
            return shifted[sy][r, N * (1 + sx):N * (1 + sx) + ROWS, columns]

        for d in range(8):
            columns = slice(d * T, (d + 1) * T)
            lhs[:, columns] = nearby(d, slice(0, T)) * gains[:, columns]
        for p, (d0, d1) in enumerate(PAIRS):
            columns = slice((8 + p) * T, (9 + p) * T)
            both = jnp.where(low(ROWS), nearby(d0, slice(T, 2 * T)), nearby(d1, slice(T, 2 * T)))
            lhs[:, columns] = both * gains[:, columns]
        near = dot(lhs[...], weights[...])
        at = pl.ds(pl.multiple_of(r * ROWS, ROWS), ROWS)
        near_a[at, :] = near[:, 0:T]
        near_h[at, :] = near[:, T:]
        return carry

    def far_block(r, carry):
        for t in range(TILES // 2):
            columns = slice(2 * t * T, 2 * (t + 1) * T)
            value = dot(adj[r], weights_t[:, columns]).astype(BF16)
            partial[N:N + ROWS, columns] = value * gains[:, columns]

        def part(x, t):
            return partial[x * N:(x + 1) * N, t * T:(t + 1) * T].astype(F32)

        for x in range(N):
            sums = {sy: None for sy in (-1, 0, 1)}
            for d, (sx, sy) in enumerate(STEPS):
                value = part(1 + x - sx, d)
                sums[sy] = value if sums[sy] is None else sums[sy] + value
            a = turn(sums[1], 1) + sums[0] + turn(sums[-1], -1)
            tops = {sy: jnp.where(low(N), part(2 + x, 9 + sy), part(x, 9 + sy)) for sy in (-1, 0, 1)}
            mid = part(1 + x, 11)
            below = tops[-1] + jnp.where(low(N), mid, 0.0)
            above = tops[1] + jnp.where(low(N), 0.0, mid)
            h = fold(turn(above, 1) + tops[0] + turn(below, -1))
            at = pl.ds(pl.multiple_of(r * ROWS + x * N, N), N)
            far_a[at, :] = a
            far_h[at, :] = h
        return carry

    def correct(v):
        for e in range(2):
            whole = jnp.concatenate(
                [recv_y[v, e].reshape(EDGE, 3 * T).astype(F32), recv_c[v, 2 * e], recv_c[v, 2 * e + 1]], axis=0
            )
            rows = EDGE + N
            a, mixed, part_a = whole[:, 0:T], whole[:, T:2 * T], whole[:, 2 * T:]
            other = turn(mixed, HALF, 1)
            h = jnp.where(low(rows), mixed, other)

            def moved(x, j):
                return jnp.concatenate([turn(x[:EDGE], -j), x[EDGE:]], axis=0)

            tiles = [moved(a, -1), a, moved(a, 1), jnp.where(low(rows), moved(h, -1), moved(h, 1)), h]
            scaled = []
            for k, tile in enumerate(tiles):
                gain_k = gains_y[e, :, k * T:(k + 1) * T]
                scaled.append((tile * spread(gain_k[0:N], gain_k[N:])).astype(BF16))
            matrix = jnp.concatenate([weights[t * T:(t + 1) * T, :] for t in Y_TILES[e]], axis=0)
            extra = dot(jnp.concatenate(scaled, axis=1), matrix)
            for ref, value in (
                (near_a, extra[:, 0:T]), (near_h, extra[:, T:]), (far_a, part_a), (far_h, other)
            ):
                y0 = e * (N - 1)
                for at, piece in (
                    (pl.ds(y0, EDGE, stride=N), value[:EDGE]),
                    (pl.ds(y0, 8, stride=ROWS), value[EDGE:EDGE + 8]),
                    (pl.ds(y0 + ROWS - N, 8, stride=ROWS), value[EDGE + 8:]),
                ):
                    ref[at, :] = ref[at, :] + piece
        for e in range(2):
            whole = recv_x[v, e].reshape(EDGE, 3 * T).astype(F32)
            a, mixed, part_a = whole[:, 0:T], whole[:, T:2 * T], whole[:, 2 * T:]
            other = turn(mixed, HALF, 1)
            h = mixed if e == 0 else other
            tiles = [turn(a, 1), a, turn(a, -1), turn(h, 1), h, turn(h, -1)]
            scaled = []
            for k, tile in enumerate(tiles):
                scaled.append((tile * spread(gains_x[e, :, k * T:(k + 1) * T])).astype(BF16))
            matrix = jnp.concatenate([weights[t * T:(t + 1) * T, :] for t in X_TILES[e]], axis=0)
            extra = dot(jnp.concatenate(scaled, axis=1), matrix)
            for ref, value in (
                (near_a, extra[:, 0:T]), (near_h, extra[:, T:]), (far_a, part_a), (far_h, other)
            ):
                for r in range(R):
                    start = r * ROWS + e * (ROWS - N)
                    ref[start:start + N, :] = ref[start:start + N, :] + value[r * N:(r + 1) * N]

    pl.semaphore_wait(barrier, 8)

    def sweep(v, carry):
        solve_edges(v)
        for copy in copies(v):
            copy.start()
        lax.fori_loop(0, R, solve_block, 0)
        lax.fori_loop(0, R, near_block, 0)
        lax.fori_loop(0, R, far_block, 0)
        for copy in copies(v):
            copy.wait_recv()
        correct(v)
        for copy in copies(v):
            copy.wait_send()
        return carry

    lax.fori_loop(0, SWEEPS, sweep, 0)

    def finish(r, carry):
        rest, back = right_sides(r)
        cur = dot(rest, solve[...]) * admit[...]
        cur_out[r] = cur[:, 0:U].astype(BF16)
        adj_out[r] = dot(back, solve_tn[...]).astype(BF16)
        return carry

    lax.fori_loop(0, R, finish, 0)


def solution(mesh):
    nx, ny = mesh.shape["gx"], mesh.shape["gy"]

    def local(inc, src, cls, slot, gain, adm, coup, sinv):
        vmem = pl.BlockSpec(memory_space=pltpu.VMEM)
        out = jax.ShapeDtypeStruct((R, ROWS, U), BF16)
        cur, adj = pl.pallas_call(
            functools.partial(kernel, nx, ny),
            out_shape=(out, out),
            in_specs=[vmem] * 8,
            out_specs=(vmem, vmem),
            scratch_shapes=[
                pltpu.VMEM((R, ROWS + 2 * N, 2 * T), BF16),
                pltpu.VMEM((R, ROWS + 2 * N, 2 * T), BF16),
                pltpu.VMEM((R, ROWS + 2 * N, 2 * T), BF16),
                pltpu.VMEM((R, ROWS, 2 * T), BF16),
                pltpu.VMEM((8 * ROWS, T), F32),
                pltpu.VMEM((8 * ROWS, T), F32),
                pltpu.VMEM((8 * ROWS, T), F32),
                pltpu.VMEM((8 * ROWS, T), F32),
                pltpu.VMEM((ROWS, TILES * T), BF16),
                pltpu.VMEM((ROWS, TILES * T), BF16),
                pltpu.VMEM((TILES * T, 2 * T), BF16),
                pltpu.VMEM((2 * T, TILES * T), BF16),
                pltpu.VMEM((ROWS + 2 * N, TILES * T), BF16),
                pltpu.VMEM((ROWS, 2 * T), F32),
                pltpu.VMEM((4 * N, 2 * T), F32),
                pltpu.VMEM((4 * EDGE, 2 * T), F32),
                pltpu.VMEM((4 * EDGE, 2 * T), F32),
                pltpu.VMEM((2, 2 * N, 5 * T), F32),
                pltpu.VMEM((2, N, 6 * T), F32),
                pltpu.VMEM((U, 2 * T), BF16),
                pltpu.VMEM((U, 2 * T), BF16),
                pltpu.VMEM((U, U), BF16),
                pltpu.VMEM((4, 8 * N, T), F32),
                pltpu.VMEM((SWEEPS, 2, R, N, 3 * T), BF16),
                pltpu.VMEM((SWEEPS, 2, R, N, 3 * T), BF16),
                pltpu.VMEM((SWEEPS, 4, 8, 3 * T), F32),
                pltpu.VMEM((SWEEPS, 2, R, N, 3 * T), BF16),
                pltpu.VMEM((SWEEPS, 2, R, N, 3 * T), BF16),
                pltpu.VMEM((SWEEPS, 4, 8, 3 * T), F32),
                pltpu.SemaphoreType.DMA((SWEEPS, 8)),
                pltpu.SemaphoreType.DMA((SWEEPS, 8)),
            ],
            compiler_params=pltpu.CompilerParams(
                collective_id=0, has_side_effects=True, vmem_limit_bytes=60 * 1024 * 1024
            ),
        )(
            inc.reshape(R, ROWS, U), src.reshape(R, ROWS, U), cls, slot, gain.reshape(64, U), adm, coup, sinv
        )
        return cur.reshape(R, N, N, U), adj.reshape(R, N, N, U)

    placed = (P(None, "gx", "gy", None), P(None, "gx", "gy", None), P("gx", "gy"), P(), P(), P(), P(), P())
    return jax.shard_map(
        local, mesh=mesh, in_specs=placed, out_specs=(placed[0], placed[0]), check_vma=False
    )
```

profile of v0, /device:TPU:0, one launch (start us, length us, event | category | flops | bytes accessed | tf_op | source)
XLA Modules:
  0.0 43.2 jit_solution(5007496012903125028)
XLA Ops:
  0.6 39.5 %shard_map.95 = (bf16[6,256,192]{2,1,0:T(8,128)(2,1)}, bf16[6,256,192]{2,1,0:T(8,128)(2,1)}) custom-call(bf16[6,256,192]{2,1,0:T(8,128)(2,1)} %bitcast.5, bf16[6,256,192]{2,1,0:T(8,128)(2,1)} %bitcast.6, s32[16,16]{1,0:T(8,128)} %cls.1, s32[8,8]{1,0:T(8,128)} %slot.1, f32[64,192]{1,0:T(8,128)} %bitcast.9, f32[8,192]{1,0:T(8,128)} %adm.1, ...), custom_call_target="tpu_custom_call" | custom-call | tf_op jit(solution)/shard_map/pallas_call | solution.py:434
  40.1 0.0 copy-start
  40.1 2.2 %copy.12 = bf16[6,16,16,192]{3,2,1,0:T(8,128)(2,1)} copy(bf16[6,16,16,192]{3,2,1,0:T(8,128)(2,1)} %bitcast.8) | data formatting | bytes 1179648
  42.3 0.0 copy-done
  42.3 0.9 %copy.13 = bf16[6,16,16,192]{3,2,1,0:T(8,128)(2,1)} copy(bf16[6,16,16,192]{3,2,1,0:T(8,128)(2,1)S(1)} %bitcast.7) | data formatting | bytes 1179648
Async XLA Ops:
  40.1 2.2 %copy-start = (bf16[6,256,192]{2,1,0:T(8,128)(2,1)S(1)}, bf16[6,256,192]{2,1,0:T(8,128)(2,1)}, u32[]{:S(2)}) copy-start(bf16[6,256,192]{2,1,0:T(8,128)(2,1)} %get-tuple-element.5) | copy-start | bytes 1769476
where the time goes:
time: 43.3 us; the launch traced here: 43.2 us
  Pallas kernels  39.5 us (91%)
  local copies, waits for them, and re-layouts  3.05 us (7%)
  between operations  0.65 us (2%)
    pallas_call x1, Pallas kernels, local(): pl.pallas_call(functools.partial(kernel, nx, ny), out_shape=(out, out), i...  39.5 us
    unnamed x4, local copies, waits for them, and re-layouts  3.05 us

commit v1 on v0

--- a/solution.py
+++ b/solution.py
@@ -16,6 +16,8 @@
 ROWS = N * N
 EDGE = R * N
 U = 192
+PER = 6
+MANY = PER * ROWS
 T = 128
 HALF = 64
 STEPS = ((-1, -1), (-1, 0), (-1, 1), (0, -1), (0, 1), (1, -1), (1, 0), (1, 1))
@@ -194,8 +196,8 @@
     for data, a_ref, h_ref, e_ref in ((inc, near_a, near_h, inc_e), (src, far_a, far_h, src_e)):
         h_ref[...] = jnp.zeros_like(h_ref)
         for r in range(R):
-            a_ref[r * ROWS:(r + 1) * ROWS, :] = data[r, :, 0:T].astype(F32)
-            h_ref[r * ROWS:(r + 1) * ROWS, 0:HALF] = data[r, :, T:U].astype(F32)
+            a_ref[r * ROWS:(r + 1) * ROWS, :] = data[r * ROWS:(r + 1) * ROWS, 0:T].astype(F32)
+            h_ref[r * ROWS:(r + 1) * ROWS, 0:HALF] = data[r * ROWS:(r + 1) * ROWS, T:U].astype(F32)
         for k, ref in enumerate((a_ref, h_ref)):
             columns = slice(k * T, (k + 1) * T)
             for e in range(2):
@@ -209,8 +211,9 @@
         for r in range(R):
             ref[r, 0:N, :] = jnp.zeros((N, 2 * T), BF16)
             ref[r, (N + 1) * N:(N + 2) * N, :] = jnp.zeros((N, 2 * T), BF16)
-    partial[0:N, :] = jnp.zeros((N, TILES * T), BF16)
-    partial[(N + 1) * N:(N + 2) * N, :] = jnp.zeros((N, TILES * T), BF16)
+    for r in range(R):
+        partial[r, 0:N, :] = jnp.zeros((N, TILES * T), BF16)
+        partial[r, (N + 1) * N:(N + 2) * N, :] = jnp.zeros((N, TILES * T), BF16)
     corner_s[...] = jnp.zeros_like(corner_s)
 
     def take(ref):
@@ -287,66 +290,80 @@
             for a, b, where, s, t in made
         ]
 
-    def right_sides(r):
-        at = pl.ds(pl.multiple_of(r * ROWS, ROWS), ROWS)
+    def right_sides(c):
+        at = pl.ds(pl.multiple_of(c * MANY, MANY), MANY)
         near = jnp.concatenate([near_a[at, :], near_h[at, 0:HALF]], axis=1)
         far = jnp.concatenate([far_a[at, :], far_h[at, 0:HALF]], axis=1)
-        rest = (inc[r].astype(F32) - near).astype(BF16)
-        back = ((src[r].astype(F32) - far) * admit[:, 0:U]).astype(BF16)
-        return rest, back
-
-    def solve_block(r, carry):
-        rest, back = right_sides(r)
-        cur = dot(rest, solve[...]) * admit[...]
-        v0[r, N:N + ROWS, :] = cur.astype(BF16)
-        vm[r, N:N + ROWS, :] = turn(cur, 1).astype(BF16)
-        vp[r, N:N + ROWS, :] = turn(cur, -1).astype(BF16)
-        adj[r] = dot(back, solve_t[...]).astype(BF16)
+        rest = (inc[at, :].astype(F32) - near).astype(BF16)
+        back = src[at, :].astype(F32) - far
+        back = [back[k * ROWS:(k + 1) * ROWS] * admit[:, 0:U] for k in range(PER)]
+        return rest, jnp.concatenate(back, axis=0).astype(BF16)
+
+    def solve_chunk(c, carry):
+        rest, back = right_sides(c)
+        cur = dot(rest, solve[...])
+        for k in range(PER):
+            r = c * PER + k
+            one_cur = cur[k * ROWS:(k + 1) * ROWS] * admit[...]
+            v0[r, N:N + ROWS, :] = one_cur.astype(BF16)
+            vm[r, N:N + ROWS, :] = turn(one_cur, 1).astype(BF16)
+            vp[r, N:N + ROWS, :] = turn(one_cur, -1).astype(BF16)
+        at = pl.ds(pl.multiple_of(c * MANY, MANY), MANY)
+        adj[at, :] = dot(back, solve_t[...]).astype(BF16)
         return carry
 
     shifted = {-1: vm, 0: v0, 1: vp}
 
-    def near_block(r, carry):
-        def nearby(d, columns):
-            sx, sy = STEPS[d]
-            return shifted[sy][r, N * (1 + sx):N * (1 + sx) + ROWS, columns]
-
-        for d in range(8):
-            columns = slice(d * T, (d + 1) * T)
-            lhs[:, columns] = nearby(d, slice(0, T)) * gains[:, columns]
-        for p, (d0, d1) in enumerate(PAIRS):
-            columns = slice((8 + p) * T, (9 + p) * T)
-            both = jnp.where(low(ROWS), nearby(d0, slice(T, 2 * T)), nearby(d1, slice(T, 2 * T)))
-            lhs[:, columns] = both * gains[:, columns]
-        near = dot(lhs[...], weights[...])
-        at = pl.ds(pl.multiple_of(r * ROWS, ROWS), ROWS)
+    def product_chunk(c, carry):
+        at = pl.ds(pl.multiple_of(c * MANY, MANY), MANY)
+        state = adj[at, :]
+        for t in range(TILES // 2):
+            columns = slice(2 * t * T, 2 * (t + 1) * T)
+            value = dot(state, weights_t[:, columns]).astype(BF16)
+            for k in range(PER):
+                partial[c * PER + k, N:N + ROWS, columns] = value[k * ROWS:(k + 1) * ROWS] * gains[:, columns]
+        for k in range(PER):
+            r = c * PER + k
+            rows = pl.ds(pl.multiple_of(r * ROWS, ROWS), ROWS)
+
+            def nearby(d, columns):
+                sx, sy = STEPS[d]
+                return shifted[sy][r, N * (1 + sx):N * (1 + sx) + ROWS, columns]
+
+            for d in range(8):
+                columns = slice(d * T, (d + 1) * T)
+                lhs[rows, columns] = nearby(d, slice(0, T)) * gains[:, columns]
+            for p, (d0, d1) in enumerate(PAIRS):
+                columns = slice((8 + p) * T, (9 + p) * T)
+                both = jnp.where(low(ROWS), nearby(d0, slice(T, 2 * T)), nearby(d1, slice(T, 2 * T)))
+                lhs[rows, columns] = both * gains[:, columns]
+        return carry
+
+    def sum_chunk(c, carry):
+        at = pl.ds(pl.multiple_of(c * MANY, MANY), MANY)
+        near = dot(lhs[at, :], weights[...])
         near_a[at, :] = near[:, 0:T]
         near_h[at, :] = near[:, T:]
-        return carry
-
-    def far_block(r, carry):
-        for t in range(TILES // 2):
-            columns = slice(2 * t * T, 2 * (t + 1) * T)
-            value = dot(adj[r], weights_t[:, columns]).astype(BF16)
-            partial[N:N + ROWS, columns] = value * gains[:, columns]
-
-        def part(x, t):
-            return partial[x * N:(x + 1) * N, t * T:(t + 1) * T].astype(F32)
-
-        for x in range(N):
-            sums = {sy: None for sy in (-1, 0, 1)}
-            for d, (sx, sy) in enumerate(STEPS):
-                value = part(1 + x - sx, d)
-                sums[sy] = value if sums[sy] is None else sums[sy] + value
-            a = turn(sums[1], 1) + sums[0] + turn(sums[-1], -1)
-            tops = {sy: jnp.where(low(N), part(2 + x, 9 + sy), part(x, 9 + sy)) for sy in (-1, 0, 1)}
-            mid = part(1 + x, 11)
-            below = tops[-1] + jnp.where(low(N), mid, 0.0)
-            above = tops[1] + jnp.where(low(N), 0.0, mid)
-            h = fold(turn(above, 1) + tops[0] + turn(below, -1))
-            at = pl.ds(pl.multiple_of(r * ROWS + x * N, N), N)
-            far_a[at, :] = a
-            far_h[at, :] = h
+        for k in range(PER):
+            r = c * PER + k
+
+            def part(x, t):
+                return partial[r, x * N:(x + 1) * N, t * T:(t + 1) * T].astype(F32)
+
+            for x in range(N):
+                sums = {sy: None for sy in (-1, 0, 1)}
+                for d, (sx, sy) in enumerate(STEPS):
+                    value = part(1 + x - sx, d)
+                    sums[sy] = value if sums[sy] is None else sums[sy] + value
+                a = turn(sums[1], 1) + sums[0] + turn(sums[-1], -1)
+                tops = {sy: jnp.where(low(N), part(2 + x, 9 + sy), part(x, 9 + sy)) for sy in (-1, 0, 1)}
+                mid = part(1 + x, 11)
+                below = tops[-1] + jnp.where(low(N), mid, 0.0)
+                above = tops[1] + jnp.where(low(N), 0.0, mid)
+                h = fold(turn(above, 1) + tops[0] + turn(below, -1))
+                rows = pl.ds(pl.multiple_of(r * ROWS + x * N, N), N)
+                far_a[rows, :] = a
+                far_h[rows, :] = h
         return carry
 
     def correct(v):
@@ -403,9 +420,9 @@
         solve_edges(v)
         for copy in copies(v):
             copy.start()
-        lax.fori_loop(0, R, solve_block, 0)
-        lax.fori_loop(0, R, near_block, 0)
-        lax.fori_loop(0, R, far_block, 0)
+        lax.fori_loop(0, R // PER, solve_chunk, 0)
+        lax.fori_loop(0, R // PER, product_chunk, 0)
+        lax.fori_loop(0, R // PER, sum_chunk, 0)
         for copy in copies(v):
             copy.wait_recv()
         correct(v)
@@ -415,14 +432,17 @@
 
     lax.fori_loop(0, SWEEPS, sweep, 0)
 
-    def finish(r, carry):
-        rest, back = right_sides(r)
-        cur = dot(rest, solve[...]) * admit[...]
-        cur_out[r] = cur[:, 0:U].astype(BF16)
-        adj_out[r] = dot(back, solve_tn[...]).astype(BF16)
+    def finish(c, carry):
+        rest, back = right_sides(c)
+        cur = dot(rest, solve[:, 0:U])
+        for k in range(PER):
+            cur_out[c * PER + k] = (cur[k * ROWS:(k + 1) * ROWS] * admit[:, 0:U]).astype(BF16)
+        value = dot(back, solve_tn[...]).astype(BF16)
+        for k in range(PER):
+            adj_out[c * PER + k] = value[k * ROWS:(k + 1) * ROWS]
         return carry
 
-    lax.fori_loop(0, R, finish, 0)
+    lax.fori_loop(0, R // PER, finish, 0)
 
 
 def solution(mesh):
@@ -440,16 +460,16 @@
                 pltpu.VMEM((R, ROWS + 2 * N, 2 * T), BF16),
                 pltpu.VMEM((R, ROWS + 2 * N, 2 * T), BF16),
                 pltpu.VMEM((R, ROWS + 2 * N, 2 * T), BF16),
-                pltpu.VMEM((R, ROWS, 2 * T), BF16),
+                pltpu.VMEM((R * ROWS, 2 * T), BF16),
                 pltpu.VMEM((8 * ROWS, T), F32),
                 pltpu.VMEM((8 * ROWS, T), F32),
                 pltpu.VMEM((8 * ROWS, T), F32),
                 pltpu.VMEM((8 * ROWS, T), F32),
                 pltpu.VMEM((ROWS, TILES * T), BF16),
-                pltpu.VMEM((ROWS, TILES * T), BF16),
+                pltpu.VMEM((R * ROWS, TILES * T), BF16),
                 pltpu.VMEM((TILES * T, 2 * T), BF16),
                 pltpu.VMEM((2 * T, TILES * T), BF16),
-                pltpu.VMEM((ROWS + 2 * N, TILES * T), BF16),
+                pltpu.VMEM((R, ROWS + 2 * N, TILES * T), BF16),
                 pltpu.VMEM((ROWS, 2 * T), F32),
                 pltpu.VMEM((4 * N, 2 * T), F32),
                 pltpu.VMEM((4 * EDGE, 2 * T), F32),
@@ -473,7 +493,7 @@
                 collective_id=0, has_side_effects=True, vmem_limit_bytes=60 * 1024 * 1024
             ),
         )(
-            inc.reshape(R, ROWS, U), src.reshape(R, ROWS, U), cls, slot, gain.reshape(64, U), adm, coup, sinv
+            inc.reshape(R * ROWS, U), src.reshape(R * ROWS, U), cls, slot, gain.reshape(64, U), adm, coup, sinv
         )
         return cur.reshape(R, N, N, U), adj.reshape(R, N, N, U)
 

time: 43.3 us -> 43 us (level)
  no operation moved by 1% of the time
where the time goes in v1:
time: 43 us; the launch traced here: 42.8 us
  Pallas kernels  39.1 us (91%)
  local copies, waits for them, and re-layouts  3.05 us (7%)
  between operations  0.65 us (2%)
    pallas_call x1, Pallas kernels, local(): pl.pallas_call(functools.partial(kernel, nx, ny), out_shape=(out, out), i...  39.1 us
    unnamed x4, local copies, waits for them, and re-layouts  3.05 us

profile of v1, /device:TPU:0, one launch (start us, length us, event | category | flops | bytes accessed | tf_op | source)
XLA Modules:
  0.0 42.8 jit_solution(4121402995006700580)
XLA Ops:
  0.6 39.1 %shard_map.95 = (bf16[6,256,192]{2,1,0:T(8,128)(2,1)}, bf16[6,256,192]{2,1,0:T(8,128)(2,1)}) custom-call(bf16[1536,192]{1,0:T(8,128)(2,1)} %bitcast.5, bf16[1536,192]{1,0:T(8,128)(2,1)} %bitcast.6, s32[16,16]{1,0:T(8,128)} %cls.1, s32[8,8]{1,0:T(8,128)} %slot.1, f32[64,192]{1,0:T(8,128)} %bitcast.9, f32[8,192]{1,0:T(8,128)} %adm.1, ...), custom_call_target="tpu_custom_call" | custom-call | tf_op jit(solution)/shard_map/pallas_call | solution.py:454
  39.7 0.0 copy-start
  39.7 2.2 %copy.12 = bf16[6,16,16,192]{3,2,1,0:T(8,128)(2,1)} copy(bf16[6,16,16,192]{3,2,1,0:T(8,128)(2,1)} %bitcast.8) | data formatting | bytes 1179648
  41.9 0.0 copy-done
  41.9 0.9 %copy.13 = bf16[6,16,16,192]{3,2,1,0:T(8,128)(2,1)} copy(bf16[6,16,16,192]{3,2,1,0:T(8,128)(2,1)S(1)} %bitcast.7) | data formatting | bytes 1179648
Async XLA Ops:
  39.7 2.2 %copy-start = (bf16[6,256,192]{2,1,0:T(8,128)(2,1)S(1)}, bf16[6,256,192]{2,1,0:T(8,128)(2,1)}, u32[]{:S(2)}) copy-start(bf16[6,256,192]{2,1,0:T(8,128)(2,1)} %get-tuple-element.5) | copy-start | bytes 1769476
